TPU v7x, 512 devices: a whole 4x8x8 slice. The times are simulated.
512 devices in a mesh: tm: 16 (over z, x_lo), lon: 32 (over x_hi, y, core).
Axes of the slice: x: 4 (x_hi: 2, x_lo: 2; x = x_hi * 2 + x_lo), y: 8, z: 8, core: 2. Of those that a mesh axis runs over, the one named last changes fastest.
Arguments:
- latent: bfloat16 [16, 32, 256, 1152], P('tm', None, 'lon'), may hold values from -6 to 6
- timestep: int32 [1], replicated, may hold values from 0 to 29
- modulation: float32 [30, 6, 1152], replicated, may hold values from -3 to 3
- window_offset: int32 [16], P('tm'), may hold values from 0 to 15
- intersection_weight: int32 [32, 32], replicated, may hold values from 1 to 9
- spatial_in: bfloat16 [1152, 1728], P('tm'), may hold values from -0.1875 to 0.1875
- spatial_gain: float32 [2, 72], replicated, may hold values from 1.2 to 2.2
- spatial_out: bfloat16 [576, 1152], P('tm'), may hold values from -0.25 to 0.25
- temporal_in: bfloat16 [1152, 1728], P('tm'), may hold values from -0.1875 to 0.1875
- temporal_gain: float32 [2, 72], replicated, may hold values from 1.2 to 2.2
- temporal_out: bfloat16 [576, 1152], P('tm'), may hold values from -0.25 to 0.25
Outputs:
- updated: bfloat16 [16, 32, 256, 1152], P('tm', None, 'lon')
All inputs are finite; a program needn't handle non-finite values.
Results may differ from a plain program's by a relative error of at most 0.02.
Values may be sent and summed in bfloat16 or wider, within the bound.
A program may use at most 128 MiB of HBM per device.

v0:
```python
import jax
import jax.numpy as jnp
from jax import lax
from jax.sharding import PartitionSpec as P

D = 1152
HEADS = 8
HEAD_DIM = 72
HD = 576
WIN = 32
STRIDE = 16


def passed_along(shard, axis, by):
    size = lax.axis_size(axis)
    return lax.ppermute(shard, axis, [(i, (i + by) % size) for i in range(size)])


def layer_norm(values):
    values = values.astype(jnp.float32)
    center = values - jnp.mean(values, axis=-1, keepdims=True)
    spread = jnp.mean(center * center, axis=-1, keepdims=True)
    return center / jnp.sqrt(spread + 1e-06)


def head_norm(projected_block, gain_row, factor):
    shaped = projected_block.reshape(projected_block.shape[:-1] + (HEADS, HEAD_DIM))
    mean_square = jnp.mean(shaped * shaped, axis=-1, keepdims=True)
    normed = shaped / jnp.sqrt(mean_square + 1e-06) * gain_row * factor
    return normed.reshape(projected_block.shape).astype(jnp.bfloat16)


def split_heads(projected, gain_table):
    queries = head_norm(projected[..., :HD], gain_table[0], HEAD_DIM ** (-0.5))
    key_rows = head_norm(projected[..., HD : 2 * HD], gain_table[1], 1.0)
    values = projected[..., 2 * HD :].astype(jnp.bfloat16)
    return (queries, key_rows, values)


def row_product(operand, weight):
    return jnp.dot(
        operand,
        lax.all_gather(weight, "tm", axis=0, tiled=True),
        preferred_element_type=jnp.float32,
    )


def frame_attention(frame_query, frame_key, frame_value):
    frames = frame_query.shape[0]
    pixels = frame_query.shape[1]
    shape_four = (frames, pixels, HEADS, HEAD_DIM)
    scores = jnp.einsum(
        "fphd,gphd->phfg",
        frame_query.reshape(shape_four),
        frame_key.reshape(shape_four),
        preferred_element_type=jnp.float32,
    )
    powers = jnp.exp(scores)
    mixture = (powers / jnp.sum(powers, axis=-1, keepdims=True)).astype(jnp.bfloat16)
    attended = jnp.einsum(
        "phfg,gphd->fphd",
        mixture,
        frame_value.reshape(shape_four),
        preferred_element_type=jnp.float32,
    )
    return attended.astype(jnp.bfloat16).reshape(frames, pixels, HD)


def local(
    latent,
    timestep,
    modulation,
    window_offset,
    intersection_weight,
    spatial_in,
    spatial_gain,
    spatial_out,
    temporal_in,
    temporal_gain,
    temporal_out,
):
    modulators = lax.dynamic_index_in_dim(modulation, timestep[0], 0, keepdims=False)
    canvas_rows = latent.shape[1]
    strip_cols = latent.shape[2]
    tokens = canvas_rows * strip_cols
    flattened = latent.reshape(tokens, D)
    normed_in = (layer_norm(flattened) * (1.0 + modulators[1]) + modulators[0]).astype(jnp.bfloat16)
    queries, key_rows, values = split_heads(row_product(normed_in, spatial_in), spatial_gain)
    own_strip = jnp.stack(
        [
            key_rows.reshape(canvas_rows, strip_cols * HD),
            values.reshape(canvas_rows, strip_cols * HD),
        ]
    )
    reach = (WIN + strip_cols - 2) // strip_cols
    from_left = []
    from_right = []
    for hop_count in range(1, reach + 1):
        from_left.append(passed_along(own_strip, "lon", hop_count))
        from_right.append(passed_along(own_strip, "lon", -hop_count))
    ordered = list(reversed(from_left)) + [own_strip] + from_right
    nearby = jnp.stack(ordered, axis=1)
    key_count = (2 * reach + 1) * tokens
    near_keys = nearby[0].reshape(key_count, HEADS, HEAD_DIM)
    near_values = nearby[1].reshape(key_count, HEADS, HEAD_DIM)
    inside = jnp.arange(strip_cols, dtype=jnp.int32)
    column = lax.axis_index("lon") * strip_cols + inside
    phase_pos = jnp.mod(column - window_offset[0], STRIDE)
    second_start = jnp.tile(inside - phase_pos, canvas_rows)
    first_start = second_start - STRIDE
    strip_shift = (jnp.arange(2 * reach + 1, dtype=jnp.int32) - reach) * strip_cols
    key_column = (
        strip_shift[:, None, None]
        + jnp.zeros((1, canvas_rows, 1), jnp.int32)
        + inside[None, None, :]
    ).reshape(key_count)
    first_mask = (
        (key_column[None, :] >= first_start[:, None])
        & (key_column[None, :] < first_start[:, None] + WIN)
    ).astype(jnp.float32)
    second_mask = (
        (key_column[None, :] >= second_start[:, None])
        & (key_column[None, :] < second_start[:, None] + WIN)
    ).astype(jnp.float32)
    weight_table = intersection_weight.astype(jnp.float32)
    positions = jnp.arange(WIN, dtype=jnp.int32)
    second_weight = jnp.sum(
        jnp.where(
            positions[None, None, :] == phase_pos[None, :, None], weight_table[:, None, :], 0.0
        ),
        axis=-1,
    ).reshape(tokens)
    first_weight = jnp.sum(
        jnp.where(
            positions[None, None, :] == phase_pos[None, :, None] + STRIDE,
            weight_table[:, None, :],
            0.0,
        ),
        axis=-1,
    ).reshape(tokens)
    first_share = first_weight / (first_weight + second_weight)
    second_share = second_weight / (first_weight + second_weight)
    head_queries = jnp.transpose(queries.reshape(tokens, HEADS, HEAD_DIM), (1, 0, 2))
    head_keys = jnp.transpose(near_keys, (1, 0, 2))
    head_values = jnp.transpose(near_values, (1, 0, 2))

    def one_head(operands):
        head_query, head_key, head_value = operands
        scores = lax.dot_general(
            head_query, head_key, (((1,), (1,)), ((), ())), preferred_element_type=jnp.float32
        )
        powers = jnp.exp(scores)
        first_total = jnp.sum(powers * first_mask, axis=1)
        second_total = jnp.sum(powers * second_mask, axis=1)
        blend = (first_share / first_total)[:, None] * first_mask + (second_share / second_total)[
            :, None
        ] * second_mask
        mixture = (powers * blend).astype(jnp.bfloat16)
        return jnp.dot(mixture, head_value, preferred_element_type=jnp.float32).astype(jnp.bfloat16)

    attended = lax.map(one_head, (head_queries, head_keys, head_values))
    spatial_result = jnp.transpose(attended, (1, 0, 2)).reshape(tokens, HD)
    middle = (
        flattened.astype(jnp.float32) + modulators[2] * row_product(spatial_result, spatial_out)
    ).astype(jnp.bfloat16)
    normed_mid = (layer_norm(middle) * (1.0 + modulators[4]) + modulators[3]).astype(jnp.bfloat16)
    frame_count = lax.axis_size("tm")
    band_rows = canvas_rows // frame_count
    pixels = band_rows * strip_cols
    own_query, own_key, own_value = split_heads(row_product(normed_mid, temporal_in), temporal_gain)
    packed = jnp.concatenate([own_query, own_key, own_value], axis=1).reshape(
        1, canvas_rows, strip_cols * 3 * HD
    )
    moved = lax.all_to_all(packed, "tm", split_axis=1, concat_axis=0, tiled=True).reshape(
        frame_count, pixels, 3 * HD
    )
    frame_query = moved[:, :, :HD]
    frame_key = moved[:, :, HD : 2 * HD]
    frame_value = moved[:, :, 2 * HD :]
    temporal_result = frame_attention(frame_query, frame_key, frame_value)
    returned = lax.all_to_all(
        temporal_result.reshape(frame_count, band_rows, strip_cols * HD),
        "tm",
        split_axis=0,
        concat_axis=1,
        tiled=True,
    )
    updated = (
        middle.astype(jnp.float32)
        + modulators[5] * row_product(returned.reshape(tokens, HD), temporal_out)
    ).astype(jnp.bfloat16)
    return updated.reshape(latent.shape)


def solution(mesh):
    in_specs = (
        P("tm", None, "lon", None),
        P(),
        P(),
        P("tm"),
        P(),
        P("tm", None),
        P(),
        P("tm", None),
        P("tm", None),
        P(),
        P("tm", None),
    )
    out_specs = P("tm", None, "lon", None)
    return jax.shard_map(local, mesh=mesh, in_specs=in_specs, out_specs=out_specs, check_vma=False)
```

profile of v0, /device:TPU:18, one launch (start us, length us, event | category | flops | bytes accessed | tf_op | source)
XLA Modules:
  0.0 489.8 jit_solution(12536033834368933591)
XLA Ops:
  20.2 95.2 %all-gather.7.cloned.1.call-done = bf16[1152,1728]{1,0:T(8,128)(2,1)} async-done(((bf16[72,1728]{1,0:T(8,128)(2,1)}), bf16[1152,1728]{1,0:T(8,128)(2,1)}) %all-gather.7.cloned.1.call-update) | async-done | bytes 3981328 | tf_op jit(solution)/shard_map/all_gather | solution.py:43
  115.4 4.0 fusion.40
  123.7 5.5 %collective-permute-start = (bf16[2,32,4608]{2,1,0:T(8,128)(2,1)S(1)}, bf16[2,32,4608]{2,1,0:T(8,128)(2,1)S(1)}, u32[]{:S(2)}, u32[]{:S(2)}) collective-permute-start(bf16[2,32,4608]{2,1,0:T(8,128)(2,1)S(1)} %constant_dynamic-update-slice_fusion), channel_id=1, source_target_pairs={{0,4},{1,5},{2,6},{3,7},{4,8},{5,9},{6,10},{7,11},{8,12},{9,13},{1... | collective-permute-start | bytes 1769480 | tf_op jit(solution)/shard_map/ppermute | solution.py:16
  130.6 60.0 %all-gather.11.cloned.1.call-done = bf16[16,36,1152]{2,1,0:T(8,128)(2,1)} async-done(((bf16[1,36,1152]{2,1,0:T(8,128)(2,1)}), bf16[16,36,1152]{2,1,0:T(8,128)(2,1)}) %all-gather.11.cloned.1.call-update) | async-done | bytes 1327120 | tf_op jit(solution)/shard_map/all_gather | solution.py:43
  190.6 3.2 reshape.319
  195.7 3.6 collective-permute-start.2
  199.3 4.3 collective-permute-start.3
  203.7 2.9 collective-permute-start.4
  207.6 8.8 %collective-permute-start.5 = (bf16[2,32,4608]{2,1,0:T(8,128)(2,1)S(1)}, bf16[2,32,4608]{2,1,0:T(8,128)(2,1)S(1)}, u32[]{:S(2)}, u32[]{:S(2)}) collective-permute-start(bf16[2,32,4608]{2,1,0:T(8,128)(2,1)S(1)} %constant_dynamic-update-slice_fusion), channel_id=1, source_target_pairs={{0,30},{1,31},{2,0},{3,1},{4,2},{5,3},{6,4},{7,5},{8,6},{9,7},{10,... | collective-permute-start | bytes 1769480 | tf_op jit(solution)/shard_map/ppermute | solution.py:16
  216.5 6.7 %collective-permute-start.6 = (bf16[2,32,4608]{2,1,0:T(8,128)(2,1)S(1)}, bf16[2,32,4608]{2,1,0:T(8,128)(2,1)S(1)}, u32[]{:S(2)}, u32[]{:S(2)}) collective-permute-start(bf16[2,32,4608]{2,1,0:T(8,128)(2,1)S(1)} %constant_dynamic-update-slice_fusion), channel_id=1, source_target_pairs={{0,29},{1,30},{2,31},{3,0},{4,1},{5,2},{6,3},{7,4},{8,5},{9,6},{10... | collective-permute-start | bytes 1769480 | tf_op jit(solution)/shard_map/ppermute | solution.py:16
  224.3 8.7 %collective-permute-done.2 = bf16[2,32,4608]{2,1,0:T(8,128)(2,1)} collective-permute-done((bf16[2,32,4608]{2,1,0:T(8,128)(2,1)S(1)}, bf16[2,32,4608]{2,1,0:T(8,128)(2,1)}, u32[]{:S(2)}, u32[]{:S(2)}) %collective-permute-start.2) | collective-permute-done | bytes 589856 | tf_op jit(solution)/shard_map/ppermute | solution.py:16
  233.0 6.5 %collective-permute-start.7 = (bf16[2,32,4608]{2,1,0:T(8,128)(2,1)S(1)}, bf16[2,32,4608]{2,1,0:T(8,128)(2,1)S(1)}, u32[]{:S(2)}, u32[]{:S(2)}) collective-permute-start(bf16[2,32,4608]{2,1,0:T(8,128)(2,1)S(1)} %constant_dynamic-update-slice_fusion), channel_id=1, source_target_pairs={{0,28},{1,29},{2,30},{3,31},{4,0},{5,1},{6,2},{7,3},{8,4},{9,5},{1... | collective-permute-start | bytes 1769480 | tf_op jit(solution)/shard_map/ppermute | solution.py:16
  241.2 32.3 %collective-permute-done.7 = bf16[2,32,4608]{2,1,0:T(8,128)(2,1)S(1)} collective-permute-done((bf16[2,32,4608]{2,1,0:T(8,128)(2,1)S(1)}, bf16[2,32,4608]{2,1,0:T(8,128)(2,1)S(1)}, u32[]{:S(2)}, u32[]{:S(2)}) %collective-permute-start.7) | collective-permute-done | bytes 589856 | tf_op jit(solution)/shard_map/ppermute | solution.py:16
  275.4 12.4 %reshape_squeeze.6 = bf16[2304,8,72]{2,1,0:T(8,128)(2,1)} reshape(bf16[1,9,32,4608]{3,2,0,1:T(8,128)(2,1)} %get-tuple-element.203) | data formatting | bytes 5308416 | tf_op jit(solution)/shard_map/reshape;squeeze | solution.py:104
  287.8 5.1 %copy.52 = bf16[8,2304,72]{2,1,0:T(8,128)(2,1)} copy(bf16[8,2304,72]{2,0,1:T(8,128)(2,1)} %bitcast.137) | data formatting | bytes 5308416
  292.9 11.6 %reshape_squeeze.7 = bf16[2304,8,72]{2,1,0:T(8,128)(2,1)} reshape(bf16[1,9,32,4608]{3,2,0,1:T(8,128)(2,1)S(1)} %get-tuple-element.202) | data formatting | bytes 5308416 | tf_op jit(solution)/shard_map/reshape;squeeze | solution.py:105
  304.4 5.2 %copy.53 = bf16[8,2304,72]{2,1,0:T(8,128)(2,1)} copy(bf16[8,2304,72]{2,0,1:T(8,128)(2,1)} %bitcast.138) | data formatting | bytes 5308416
  309.6 37.1 %while.12 = (s32[]{:T(128)}, bf16[8,256,72]{1,2,0:T(8,128)(2,1)S(1)}, bf16[8,256,72]{2,1,0:T(8,128)(2,1)}, bf16[8,2304,72]{2,1,0:T(8,128)(2,1)}, f32[256]{0:T(25...) while((s32[]{:T(128)}, ...), condition=%wide.region_9.10_spmd.clone.clone, body=%wide.region_6.9_spmd.clone.clone.sunk | while | flops 182274048 | bytes 6042749 | solution.py:161
  309.6 2.5 select_reduce_fusion.5
  314.3 2.4 select_reduce_fusion.5
  323.6 2.4 select_reduce_fusion.5
  332.8 2.4 select_reduce_fusion.5
  347.8 4.1 fusion.42
  360.6 5.1 %reshape.322 = bf16[1,32,13824]{2,0,1:T(2,128)(2,1)S(1)} reshape(bf16[256,1728]{1,0:T(8,128)(2,1)} %copy.54) | data formatting | bytes 1769472 | tf_op jit(solution)/shard_map/reshape | solution.py:171
  366.2 6.9 %reduce.16 = bf16[32,13824]{1,0:T(8,128)(2,1)} reduce(bf16[32,1,13824]{2,1,0:T(2,128)(2,1)S(1)} %bitcast.139, bf16[]{:T(256)} %broadcast.350), dimensions={1}, to_apply=%bitcast.111.reduce_sub_computation | reduce | bytes 1769474
  373.1 3.0 reshape.330
  376.2 6.0 %all-to-all-start = ((bf16[16,2,13824]{2,1,0:T(2,128)(2,1)}), bf16[16,2,13824]{2,1,0:T(2,128)(2,1)}, u32[]{:S(2)}, u32[]{:S(2)}) async-start(bf16[16,2,13824]{2,1,0:T(2,128)(2,1)} %reshape.330), calls=%async_computation | async-start | bytes 1769472 | tf_op jit(solution)/shard_map/all_to_all | solution.py:174
  382.8 24.2 %all-to-all-done = bf16[16,2,13824]{2,1,0:T(2,128)(2,1)} async-done(((bf16[16,2,13824]{2,1,0:T(2,128)(2,1)}), bf16[16,2,13824]{2,1,0:T(2,128)(2,1)}, u32[]{:S(2)}, u32[]{:S(2)}) %all-to-all-start) | async-done | bytes 884768 | tf_op jit(solution)/shard_map/all_to_all | solution.py:174
  407.0 4.3 reshape.331
  411.3 6.0 %bitcast_reduce_fusion = bf16[32,13824]{1,0:T(8,128)(2,1)} fusion(bf16[32,1,13824]{2,1,0:T(2,128)(2,1)S(1)} %reshape.331), kind=kLoop, calls=%fused_computation.135 | loop fusion | bytes 1769472 | tf_op jit(solution)/shard_map/all_to_all | solution.py:174
  428.0 4.8 all-to-all-start.1
  432.8 46.2 %all-gather.13.cloned.1.call-done = bf16[16,36,1152]{2,1,0:T(8,128)(2,1)} async-done(((bf16[1,36,1152]{2,1,0:T(8,128)(2,1)}), bf16[16,36,1152]{2,1,0:T(8,128)(2,1)}) %all-gather.13.cloned.1.call-update) | async-done | bytes 1327120 | tf_op jit(solution)/shard_map/all_gather | solution.py:43
  (144 shorter events, 78.2 us)
Async XLA Ops:
  6.5 108.9 %copy-start = (bf16[1,32,8,1152]{3,2,1,0:T(8,128)(2,1)S(1)}, bf16[1,32,8,1152]{3,2,1,0:T(8,128)(2,1)}, u32[]{:S(2)}) copy-start(bf16[1,32,8,1152]{3,2,1,0:T(8,128)(2,1)} %param.13) | copy-start | bytes 1769476
  6.5 108.8 %all-gather.7.cloned.1.call-start = ((), (), s32[]{:S(2)}) async-start(), calls=%async_computation.2 | async-start | bytes 4386816 | tf_op jit(solution)/shard_map/all_gather | solution.py:43
  7.3 183.3 %all-gather.11.cloned.1.call-start = ((), (), s32[]{:S(2)}) async-start(), calls=%async_computation.4 | async-start | bytes 1566720 | tf_op jit(solution)/shard_map/all_gather | solution.py:43
  8.0 339.8 %all-gather.9.cloned.1.call-start = ((), (), s32[]{:S(2)}) async-start(), calls=%async_computation.3 | async-start | bytes 4386816 | tf_op jit(solution)/shard_map/all_gather | solution.py:43
  120.9 2.2 copy-start.2
  121.7 7.5 %copy-start.8 = (f32[2,72]{1,0:T(2,128)S(1)}, f32[2,72]{1,0:T(2,128)}, u32[]{:S(2)}) copy-start(f32[2,72]{1,0:T(2,128)} %param.22) | copy-start | bytes 1732
  121.7 8.8 %copy-start.5 = (s32[256]{0:T(256)S(1)}, s32[256]{0:T(256)}, u32[]{:S(2)}) copy-start(s32[256]{0:T(256)} %tile.10) | copy-start | bytes 3076
  121.7 8.8 %copy-start.6 = (f32[256]{0:T(256)S(1)}, f32[256]{0:T(256)}, u32[]{:S(2)}) copy-start(f32[256]{0:T(256)} %reshape.307) | copy-start | bytes 3076
  121.7 8.8 %copy-start.7 = (f32[256]{0:T(256)S(1)}, f32[256]{0:T(256)}, u32[]{:S(2)}) copy-start(f32[256]{0:T(256)} %reshape.308) | copy-start | bytes 3076
  123.7 84.0 %collective-permute-start = (bf16[2,32,4608]{2,1,0:T(8,128)(2,1)S(1)}, bf16[2,32,4608]{2,1,0:T(8,128)(2,1)S(1)}, u32[]{:S(2)}, u32[]{:S(2)}) collective-permute-start(bf16[2,32,4608]{2,1,0:T(8,128)(2,1)S(1)} %constant_dynamic-update-slice_fusion), channel_id=1, source_target_pairs={{0,4},{1,5},{2,6},{3,7},{4,8},{5,9},{6,10},{7,11},{8,12},{9,13},{1... | collective-permute-start | bytes 1769480 | tf_op jit(solution)/shard_map/ppermute | solution.py:16
  193.8 22.7 %collective-permute-start.1 = (bf16[2,32,4608]{2,1,0:T(8,128)(2,1)S(1)}, bf16[2,32,4608]{2,1,0:T(8,128)(2,1)}, u32[]{:S(2)}, u32[]{:S(2)}) collective-permute-start(bf16[2,32,4608]{2,1,0:T(8,128)(2,1)S(1)} %constant_dynamic-update-slice_fusion), channel_id=1, source_target_pairs={{0,3},{1,4},{2,5},{3,6},{4,7},{5,8},{6,9},{7,10},{8,11},{9,12},{10... | collective-permute-start | bytes 1769480 | tf_op jit(solution)/shard_map/ppermute | solution.py:16
  195.7 37.3 %collective-permute-start.2 = (bf16[2,32,4608]{2,1,0:T(8,128)(2,1)S(1)}, bf16[2,32,4608]{2,1,0:T(8,128)(2,1)}, u32[]{:S(2)}, u32[]{:S(2)}) collective-permute-start(bf16[2,32,4608]{2,1,0:T(8,128)(2,1)S(1)} %constant_dynamic-update-slice_fusion), channel_id=1, source_target_pairs={{0,2},{1,3},{2,4},{3,5},{4,6},{5,7},{6,8},{7,9},{8,10},{9,11},{10,... | collective-permute-start | bytes 1769480 | tf_op jit(solution)/shard_map/ppermute | solution.py:16
  199.3 41.2 %collective-permute-start.3 = (bf16[2,32,4608]{2,1,0:T(8,128)(2,1)S(1)}, bf16[2,32,4608]{2,1,0:T(8,128)(2,1)S(1)}, u32[]{:S(2)}, u32[]{:S(2)}) collective-permute-start(bf16[2,32,4608]{2,1,0:T(8,128)(2,1)S(1)} %constant_dynamic-update-slice_fusion), channel_id=1, source_target_pairs={{0,1},{1,2},{2,3},{3,4},{4,5},{5,6},{6,7},{7,8},{8,9},{9,10},{10,1... | collective-permute-start | bytes 1769480 | tf_op jit(solution)/shard_map/ppermute | solution.py:16
  203.7 37.0 %collective-permute-start.4 = (bf16[2,32,4608]{2,1,0:T(8,128)(2,1)S(1)}, bf16[2,32,4608]{2,1,0:T(8,128)(2,1)S(1)}, u32[]{:S(2)}, u32[]{:S(2)}) collective-permute-start(bf16[2,32,4608]{2,1,0:T(8,128)(2,1)S(1)} %constant_dynamic-update-slice_fusion), channel_id=1, source_target_pairs={{0,31},{1,0},{2,1},{3,2},{4,3},{5,4},{6,5},{7,6},{8,7},{9,8},{10,9... | collective-permute-start | bytes 1769480 | tf_op jit(solution)/shard_map/ppermute | solution.py:16
  207.6 33.1 %collective-permute-start.5 = (bf16[2,32,4608]{2,1,0:T(8,128)(2,1)S(1)}, bf16[2,32,4608]{2,1,0:T(8,128)(2,1)S(1)}, u32[]{:S(2)}, u32[]{:S(2)}) collective-permute-start(bf16[2,32,4608]{2,1,0:T(8,128)(2,1)S(1)} %constant_dynamic-update-slice_fusion), channel_id=1, source_target_pairs={{0,30},{1,31},{2,0},{3,1},{4,2},{5,3},{6,4},{7,5},{8,6},{9,7},{10,... | collective-permute-start | bytes 1769480 | tf_op jit(solution)/shard_map/ppermute | solution.py:16
  216.5 24.6 %collective-permute-start.6 = (bf16[2,32,4608]{2,1,0:T(8,128)(2,1)S(1)}, bf16[2,32,4608]{2,1,0:T(8,128)(2,1)S(1)}, u32[]{:S(2)}, u32[]{:S(2)}) collective-permute-start(bf16[2,32,4608]{2,1,0:T(8,128)(2,1)S(1)} %constant_dynamic-update-slice_fusion), channel_id=1, source_target_pairs={{0,29},{1,30},{2,31},{3,0},{4,1},{5,2},{6,3},{7,4},{8,5},{9,6},{10... | collective-permute-start | bytes 1769480 | tf_op jit(solution)/shard_map/ppermute | solution.py:16
  233.0 40.5 %collective-permute-start.7 = (bf16[2,32,4608]{2,1,0:T(8,128)(2,1)S(1)}, bf16[2,32,4608]{2,1,0:T(8,128)(2,1)S(1)}, u32[]{:S(2)}, u32[]{:S(2)}) collective-permute-start(bf16[2,32,4608]{2,1,0:T(8,128)(2,1)S(1)} %constant_dynamic-update-slice_fusion), channel_id=1, source_target_pairs={{0,28},{1,29},{2,30},{3,31},{4,0},{5,1},{6,2},{7,3},{8,4},{9,5},{1... | collective-permute-start | bytes 1769480 | tf_op jit(solution)/shard_map/ppermute | solution.py:16
  304.4 5.2 %copy-start.3 = (bf16[8,256,72]{1,2,0:T(8,128)(2,1)S(1)}, bf16[8,256,72]{1,2,0:T(8,128)(2,1)}, u32[]{:S(2)}) copy-start(bf16[8,256,72]{1,2,0:T(8,128)(2,1)} %custom-call.2) | copy-start | bytes 884740
  304.4 5.2 %copy-start.4 = (s32[2304]{0:T(1024)S(1)}, s32[2304]{0:T(1024)}, u32[]{:S(2)}) copy-start(s32[2304]{0:T(1024)} %add.226) | copy-start | bytes 27652
  309.6 37.1 %copy-start.1 = (bf16[576,1152]{1,0:T(8,128)(2,1)S(1)}, bf16[576,1152]{1,0:T(8,128)(2,1)}, u32[]{:S(2)}) copy-start(bf16[576,1152]{1,0:T(8,128)(2,1)} %reshape.319) | copy-start | bytes 3981316
  376.2 30.9 %all-to-all-start = ((bf16[16,2,13824]{2,1,0:T(2,128)(2,1)}), bf16[16,2,13824]{2,1,0:T(2,128)(2,1)}, u32[]{:S(2)}, u32[]{:S(2)}) async-start(bf16[16,2,13824]{2,1,0:T(2,128)(2,1)} %reshape.330), calls=%async_computation | async-start | bytes 1769472 | tf_op jit(solution)/shard_map/all_to_all | solution.py:174
  382.2 96.8 %all-gather.13.cloned.1.call-start = ((), (), s32[]{:S(2)}) async-start(), calls=%async_computation.5 | async-start | bytes 1566720 | tf_op jit(solution)/shard_map/all_gather | solution.py:43
  428.0 53.2 %all-to-all-start.1 = ((bf16[16,2,4608]{2,1,0:T(2,128)(2,1)}), bf16[16,2,4608]{2,1,0:T(2,128)(2,1)S(1)}, u32[]{:S(2)}, u32[]{:S(2)}) async-start(bf16[16,2,4608]{2,1,0:T(2,128)(2,1)} %reshape_reshape.3), calls=%async_computation.1 | async-start | bytes 589824 | tf_op jit(solution)/shard_map/all_to_all | solution.py:181
Sparse Core Ops, SparseCore 0:
  9.4 105.8 all-gather.6
  117.5 73.0 all-gather.10
  192.7 106.0 all-gather.8
  384.8 94.0 all-gather.12
where the time goes:
time: 497 us; the launch traced here: 490 us
  waiting for transfers between devices  270 us (54%)
  local copies, waits for them, and re-layouts  82.6 us (17%)
  starting transfers between devices  51.2 us (10%)
  matrix products  49.5 us (10%)
  other arithmetic  21.5 us (4%)
  between operations  15.2 us (3%)
    all_gather x4, waiting for transfers between devices, row_product(): lax.all_gather(weight, 'tm', axis=0, tiled=True)  201 us
    ppermute x8, waiting for transfers between devices, passed_along(): lax.ppermute(shard, axis, [(i, (i + by) % size) for i in range(size)])  41.3 us
    ppermute x8, starting transfers between devices, passed_along(): lax.ppermute(shard, axis, [(i, (i + by) % size) for i in range(size)])  40.3 us
    unnamed x34, local copies, waits for them, and re-layouts  26 us
    all_to_all x1, waiting for transfers between devices, local(): lax.all_to_all(packed, 'tm', split_axis=1, concat_axis=0, tiled=True)  24.2 us
    dot_general x8, matrix products, one_head(): lax.dot_general(head_query, head_key, (((1,), (1,)), ((), ())), preferred...  19.2 us
    dot_general x8, matrix products, one_head(): jnp.dot(mixture, head_value, preferred_element_type=jnp.float32)  17.6 us
    another operation x1, local copies, waits for them, and re-layouts, local(): near_keys = nearby[0].reshape(key_count, HEADS, HEAD_DIM)  12.4 us
  transfers between devices with their start and end apart: 14, of which 7 were waited for; matrix products, arithmetic and copies ran while one was open for 25% of the time, Pallas kernels for 0%

commit v1 on v0

v1 whole, which is shorter than its diff:
```python
import functools
import math

import jax
import jax.numpy as jnp
from jax import lax
from jax.experimental import pallas as pl
from jax.experimental.pallas import tpu as pltpu
from jax.sharding import PartitionSpec as P

D = 1152
HEADS = 8
HEAD_DIM = 72
HD = 576
HP = 640
ROWS = 32
COLS = 8
TOK = ROWS * COLS
WIN = 32
STRIDE = 16
BF = jnp.bfloat16
F32 = jnp.float32
MESH = pl.DeviceIdType.MESH
LOG2E = math.log2(math.e)


def iota(shape, dim):
    return lax.broadcasted_iota(jnp.int32, shape, dim)


def dot(a, b):
    return jnp.dot(a, b, preferred_element_type=F32)


def dot_t(a, b):
    return lax.dot_general(a, b, (((1,), (1,)), ((), ())), preferred_element_type=F32)


def layer_norm(x):
    center = x - jnp.mean(x, axis=-1, keepdims=True)
    spread = jnp.mean(center * center, axis=-1, keepdims=True)
    return center * lax.rsqrt(spread + 1e-06)


def head_norm(p, gain, seg, seg_t):
    square = dot((p * p).astype(BF), seg) * (1.0 / HEAD_DIM) + 1e-06
    inverse = lax.rsqrt(square)
    high = inverse.astype(BF)
    low = (inverse - high.astype(F32)).astype(BF)
    spread = dot(jnp.concatenate([high, low], axis=1), seg_t)
    return (p * spread * gain).astype(BF)


def kernel(
    lat_ref, ts_ref, mod_ref, off_ref, iw_ref, si_ref, sg_ref, so_ref, ti_ref, tg_ref, to_ref,
    out_ref,
    w_si, w_so, w_ti, w_to, w_spat, w_temp, wo_spat, wo_temp,
    seg, seg_t, gains, gpad, latp, xs, qbuf, kbuf, vbuf, kcell, vcell, att, mid, nm, xt, tqkv, tsend, rt,
    w_send, w_recv, s_send, s_recv, kv_send, kv_recv, a_send, a_recv, r_send, r_recv, loc,
):
    t = lax.axis_index("tm")
    l = lax.axis_index("lon")
    nlon = lax.axis_size("lon")
    ntm = lax.axis_size("tm")
    nz, nq = ntm // 2, nlon // 2
    ny = nq // 2
    z, xl = t // 2, lax.rem(t, 2)
    q, c = l // 2, lax.rem(l, 2)
    xh, y = q // ny, lax.rem(q, ny)
    d = 1 - 2 * c

    def dev(tm, lon):
        return {"tm": tm, "lon": lon}

    def around(step):
        x = lax.rem(xh * 2 + xl + step + 4, 4)
        return dev(z * 2 + lax.rem(x, 2), ((x // 2) * ny + y) * 2 + c)

    zn = dev(lax.rem(z + d + nz, nz) * 2 + xl, l)
    xn = around(d)
    xp = around(-d)
    sib = dev(t, q * 2 + 1 - c)
    east = dev(t, lax.rem(q + 1, nq) * 2 + c)
    west = dev(t, lax.rem(q + nq - 1, nq) * 2 + c)

    barrier = pltpu.get_barrier_semaphore()
    others = [dev(lax.rem(t + k, ntm), l) for k in range(1, 16)] + [sib, east, west]
    across_x = lax.rem(xh * 2 + xl + jnp.where(xl == 0, 3, 1), 4)
    across = dev(z * 2 + lax.rem(across_x, 2), ((across_x // 2) * ny + y) * 2 + c)
    others.append(across)
    for other in others:
        pl.semaphore_signal(barrier, inc=1, device_id=other, device_id_type=MESH)

    weights = (w_si, w_so, w_ti, w_to)
    sources = (si_ref, so_ref, ti_ref, to_ref)
    own = [pltpu.make_async_copy(sources[a], weights[a].at[t], loc.at[a]) for a in range(4)]
    for copy in own:
        copy.start()

    pl.semaphore_wait(barrier, len(others))

    sent = []

    def wcopy(a, slot, sem, target):
        return pltpu.make_async_remote_copy(
            src_ref=weights[a].at[slot], dst_ref=weights[a].at[slot],
            send_sem=w_send.at[a, sem], recv_sem=w_recv.at[a, slot],
            device_id=target, device_id_type=MESH,
        )

    def mine(i, plane):
        return lax.rem(z - d * (i + c) + 2 * nz, nz) * 2 + plane

    def theirs(i, plane):
        return lax.rem(z + d * (i + 1 - c) + 2 * nz, nz) * 2 + plane

    def send(a, slot, sem, target):
        copy = wcopy(a, slot, sem, target)
        copy.start()
        sent.append(copy)

    def gather_start(a):
        own[a].wait()

        @pl.when(c == 1)
        def _():
            wcopy(a, t, 3, zn).start()

    def gather_a(a, i):
        slot = mine(i, xl)
        if i == 0:

            @pl.when(c == 1)
            def _():
                wcopy(a, slot, 0, zn).wait_recv()
                wcopy(a, slot, 8, sib).start()

        else:
            wcopy(a, slot, 0, zn).wait_recv()
            send(a, slot, 8 + i, sib)
        if i < 3:
            send(a, slot, i, zn)
        send(a, slot, 4 + i, xn)

    def gather_b(a, i):
        slot = mine(i, 1 - xl)
        wcopy(a, slot, 0, zn).wait_recv()
        send(a, slot, 12 + i, sib)

    def gather_rest(a):
        for i in range(4):
            slot = theirs(i, xl)
            if i == 0:

                @pl.when(c == 0)
                def _():
                    wcopy(a, slot, 0, zn).wait_recv()

            else:
                wcopy(a, slot, 0, zn).wait_recv()
            wcopy(a, theirs(i, 1 - xl), 0, zn).wait_recv()

    def gather_end(a):
        @pl.when(c == 1)
        def _():
            wcopy(a, t, 3, zn).wait_send()
            wcopy(a, mine(0, xl), 8, sib).wait_send()

    def arrange_in(source, target):
        @pl.loop(0, 8)
        def _(pair):
            rows = pl.ds(pl.multiple_of(pair * 144, 16), 144)
            both = jnp.concatenate(
                [source[2 * pair].astype(F32), source[2 * pair + 1].astype(F32)], axis=0
            )
            for part in range(3):
                cut = both[:, part * HD : (part + 1) * HD]
                wide = jnp.concatenate([cut, jnp.zeros((144, HP - HD), F32)], axis=1)
                target[part, rows, :] = wide.astype(BF)

    def arrange_out(source, target):
        for four in range(4):
            block = jnp.concatenate([source[4 * four + k].astype(F32) for k in range(4)], axis=0)
            target[144 * four : 144 * (four + 1), :] = block.astype(BF)
        target[HD:HP, :] = jnp.zeros((HP - HD, D), BF)

    gather_start(0)
    gather_a(0, 0)

    steps = mod_ref.shape[0]
    chosen = (iota((steps, 6, D), 0) == ts_ref[0]).astype(F32)
    modulators = jnp.sum(mod_ref[...] * chosen, axis=0)
    there = iota((TOK, TOK), 1)
    here = iota((TOK, TOK), 0)
    perm = (there == (here & 31) * COLS + (here >> 5)).astype(F32).astype(BF)
    ordered = dot(perm, lat_ref[...])
    latp[...] = ordered.astype(BF)
    xs[2] = (layer_norm(ordered) * (1.0 + modulators[1:2]) + modulators[0:1]).astype(BF)

    HALF = TOK // 2

    def scopy(source, hop, side, half):
        part = pl.ds(half * HALF, HALF)
        slot = 2 - hop if side == 0 else 2 + hop
        return pltpu.make_async_remote_copy(
            src_ref=xs.at[source, part], dst_ref=xs.at[slot, part],
            send_sem=s_send.at[2 * (hop - 1) + side, half],
            recv_sem=s_recv.at[2 * (hop - 1) + side, half],
            device_id=east if side == 0 else west, device_id_type=MESH,
        )

    def strip_send(hop, half):
        for side in (0, 1):
            source = 2 if hop == 1 else (1 if side == 0 else 3)
            if hop == 2:
                scopy(2, 1, side, half).wait_recv()
            copy = scopy(source, hop, side, half)
            copy.start()
            sent.append(copy)

    strip_send(1, 0)
    strip_send(1, 1)

    kbuf[9 * COLS :] = jnp.zeros((COLS, ROWS, HP), BF)
    vbuf[9 * COLS :] = jnp.zeros((COLS, ROWS, HP), BF)

    lane = iota((HP, 128), 0)
    head = iota((HP, 128), 1) * HEAD_DIM
    seg[...] = ((lane >= head) & (lane < head + HEAD_DIM)).astype(F32).astype(BF)
    lane = iota((256, HP), 1)
    head = (iota((256, HP), 0) & 127) * HEAD_DIM
    seg_t[...] = ((lane >= head) & (lane < head + HEAD_DIM)).astype(F32).astype(BF)
    gpad[...] = jnp.zeros_like(gpad)
    gpad[0:2, 0:HEAD_DIM] = sg_ref[...]
    gpad[2:4, 0:HEAD_DIM] = tg_ref[...]
    lane = iota((128, HP), 1)
    within = lane
    for h in range(1, HEADS):
        within = jnp.where(lane >= h * HEAD_DIM, lane - h * HEAD_DIM, within)
    spread = (within == iota((128, HP), 0)).astype(F32)
    gains[...] = jnp.dot(
        gpad[...], spread, preferred_element_type=F32, precision=lax.Precision.HIGHEST
    )
    factor = HEAD_DIM ** (-0.5) * LOG2E

    gather_a(0, 1)
    gather_b(0, 0)
    gather_a(0, 2)
    gather_b(0, 1)
    strip_send(2, 0)
    gather_a(0, 3)
    gather_b(0, 2)
    gather_start(1)
    gather_a(1, 0)
    strip_send(2, 1)
    gather_b(0, 3)
    gather_a(1, 1)
    gather_b(1, 0)
    gather_a(1, 2)
    gather_b(1, 1)
    gather_rest(0)
    gather_start(2)
    gather_start(3)
    gather_a(2, 0)
    gather_a(3, 0)
    arrange_in(w_si, w_spat)

    qbuf[...] = head_norm(dot(xs[2], w_spat[0]), gains[0:1] * factor, seg[...], seg_t[...])
    gather_a(1, 3)
    gather_b(1, 2)

    def keys_values(slot):
        cols = pl.ds(slot * (2 * COLS), COLS)
        x = xs[slot]
        keys = head_norm(dot(x, w_spat[1]), gains[1:2], seg[...], seg_t[...])
        kbuf[cols] = keys.reshape(COLS, ROWS, HP)
        vbuf[cols] = dot(x, w_spat[2]).astype(BF).reshape(COLS, ROWS, HP)

    def kv_copies(order):
        target = 2 * order + 1
        source = target + 1 - 2 * c
        src = pl.ds(source * COLS, COLS)
        dst = pl.ds(target * COLS, COLS)
        return [
            pltpu.make_async_remote_copy(
                src_ref=buf.at[src], dst_ref=buf.at[dst], send_sem=kv_send.at[j, order],
                recv_sem=kv_recv.at[j, order], device_id=sib, device_id_type=MESH,
            )
            for j, buf in enumerate((kbuf, vbuf))
        ]

    def kv_share(order):
        for copy in kv_copies(order):
            copy.start()
            sent.append(copy)

    @pl.loop(0, 3)
    def _(i):
        keys_values(2 - lax.rem(i, 2) + i // 2)

    kv_share(1)
    kv_share(2)
    kv_share(3 * c)
    gather_b(1, 3)
    gather_rest(1)
    arrange_out(w_so, wo_spat)
    gather_a(2, 1)
    gather_a(3, 1)
    gather_b(2, 0)
    gather_b(3, 0)
    for half in (0, 1):
        for side in (0, 1):
            scopy(2, 2, side, half).wait_recv()

    @pl.loop(0, 2)
    def _(i):
        keys_values(4 * i)

    kv_share(3 - 3 * c)
    gather_a(2, 2)
    gather_a(3, 2)
    gather_b(2, 1)
    gather_b(3, 1)

    shift = lax.rem(COLS * l - off_ref[0] + STRIDE, STRIDE)
    table = iw_ref[...].astype(F32)
    place = iota((ROWS, WIN), 1)
    second, first = [], []
    for col in range(COLS):
        m = lax.rem(shift + col, STRIDE)
        second.append(jnp.sum(jnp.where(place == m, table, 0.0), axis=1, keepdims=True))
        first.append(jnp.sum(jnp.where(place == m + STRIDE, table, 0.0), axis=1, keepdims=True))
    second = jnp.concatenate(second, axis=0)
    first = jnp.concatenate(first, axis=0)
    share_first = first / (first + second)
    share_second = second / (first + second)
    early = (shift + (iota((TOK, 1), 0) >> 5)) < STRIDE

    for order in range(4):
        for copy in kv_copies(order):
            copy.wait_recv()

    CELL = STRIDE * ROWS
    for col in range(4 * STRIDE):
        rows = slice(col * ROWS, (col + 1) * ROWS)
        kcell[rows, :] = kbuf[col + STRIDE - shift]
        vcell[rows, :] = vbuf[col + STRIDE - shift]

    def window(h):
        w = pl.multiple_of(((9 * h) // 16) * 128, 128)
        off = HEAD_DIM * h - w
        lanes = iota((1, 256), 1)
        inside = ((lanes >= off) & (lanes < off + HEAD_DIM)).astype(F32)
        return w, inside

    def spatial_head(h, _):
        w, inside = window(h)
        cols = pl.ds(w, 256)
        inside_b = inside.astype(BF)
        outside_b = (1.0 - inside).astype(BF)
        qh = qbuf[:, cols] * inside_b
        totals, sums = [], []
        for g in range(4):
            rows = slice(g * CELL, (g + 1) * CELL)
            powers = jnp.exp2(dot_t(qh, kcell[rows, cols])).astype(BF)
            o = dot(powers, vcell[rows, cols] * inside_b + outside_b)
            totals.append(o)
            sums.append(o[:, 255:256])
        near = sums[1] + sums[2]
        ca = share_first / jnp.where(early, sums[0] + sums[1], near)
        cb = share_second / jnp.where(early, near, sums[2] + sums[3])
        cab = ca + cb
        res = (
            jnp.where(early, ca, 0.0) * totals[0]
            + jnp.where(early, cab, ca) * totals[1]
            + jnp.where(early, cb, cab) * totals[2]
            + jnp.where(early, 0.0, cb) * totals[3]
        )
        att[:, cols] = att[:, cols] * (1.0 - inside) + res * inside
        return 0

    att[...] = jnp.zeros_like(att)
    lax.fori_loop(0, 4, spatial_head, 0)
    gather_a(2, 3)
    gather_a(3, 3)
    gather_b(2, 2)
    gather_b(3, 2)
    lax.fori_loop(4, 8, spatial_head, 0)
    gather_b(2, 3)
    gather_b(3, 3)

    middle = latp[...].astype(F32) + modulators[2:3] * dot(att[...].astype(BF), wo_spat[...])
    middle = middle.astype(BF)
    mid[...] = middle
    normed = layer_norm(middle.astype(F32)) * (1.0 + modulators[4:5]) + modulators[3:4]
    nm[...] = normed.astype(BF)

    BAND = TOK // 16
    ORDER = (8, 9, 7, 10, 6, 11, 5, 12, 4, 13, 3, 14, 2, 15, 1)

    def band(index):
        return pl.ds(pl.multiple_of(index * BAND, BAND), BAND)

    def exchange(source, target, send_sems, recv_sems):
        for k in ORDER:
            peer = lax.rem(t + k, ntm)
            copy = pltpu.make_async_remote_copy(
                src_ref=source.at[band(peer)], dst_ref=target.at[band(t)],
                send_sem=send_sems.at[k], recv_sem=recv_sems.at[t],
                device_id=dev(peer, l), device_id_type=MESH,
            )
            copy.start()
            sent.append(copy)
        target[band(t), :] = source[band(t), :]

    def exchange_wait(source, target, send_sems, recv_sems):
        for k in range(1, 16):
            peer = lax.rem(t + k, ntm)
            pltpu.make_async_remote_copy(
                src_ref=source.at[band(peer)], dst_ref=target.at[band(peer)],
                send_sem=send_sems.at[k], recv_sem=recv_sems.at[peer],
                device_id=dev(peer, l), device_id_type=MESH,
            ).wait_recv()

    exchange(nm, xt, a_send, a_recv)
    gather_rest(2)
    gather_rest(3)
    arrange_in(w_ti, w_temp)
    arrange_out(w_to, wo_temp)
    exchange_wait(nm, xt, a_send, a_recv)

    x = xt[...]
    tqkv[0] = head_norm(dot(x, w_temp[0]), gains[2:3] * factor, seg[...], seg_t[...])
    tqkv[1] = head_norm(dot(x, w_temp[1]), gains[3:4], seg[...], seg_t[...])
    tqkv[2] = dot(x, w_temp[2]).astype(BF)
    same = ((iota((TOK, TOK), 0) & 15) == (iota((TOK, TOK), 1) & 15)).astype(F32)

    def temporal_head(h, _):
        w, inside = window(h)
        cols = pl.ds(w, 256)
        inside_b = inside.astype(BF)
        outside_b = (1.0 - inside).astype(BF)
        scores = dot_t(tqkv[0, :, cols] * inside_b, tqkv[1, :, cols])
        powers = (jnp.exp2(scores) * same).astype(BF)
        o = dot(powers, tqkv[2, :, cols] * inside_b + outside_b)
        att[:, cols] = att[:, cols] * (1.0 - inside) + o * (inside / o[:, 255:256])
        return 0

    att[...] = jnp.zeros_like(att)
    lax.fori_loop(0, 8, temporal_head, 0)
    tsend[...] = att[...].astype(BF)
    exchange(tsend, rt, r_send, r_recv)
    there = iota((TOK, TOK), 1)
    here = iota((TOK, TOK), 0)
    back = (there == (here & 7) * ROWS + (here >> 3)).astype(F32).astype(BF)
    exchange_wait(tsend, rt, r_send, r_recv)

    result = mid[...].astype(F32) + modulators[5:6] * dot(rt[...], wo_temp[...])
    out_ref[...] = dot(back, result.astype(BF)).astype(BF)

    for copy in sent:
        copy.wait_send()
    for a in range(4):
        gather_end(a)


def local(
    latent,
    timestep,
    modulation,
    window_offset,
    intersection_weight,
    spatial_in,
    spatial_gain,
    spatial_out,
    temporal_in,
    temporal_gain,
    temporal_out,
):
    vmem = pl.BlockSpec(memory_space=pltpu.VMEM)
    smem = pl.BlockSpec(memory_space=pltpu.SMEM)
    hbm = pl.BlockSpec(memory_space=pl.ANY)
    dma = pltpu.SemaphoreType.DMA
    out = pl.pallas_call(
        kernel,
        out_shape=jax.ShapeDtypeStruct((TOK, D), BF),
        in_specs=[vmem, smem, vmem, smem, vmem, hbm, vmem, hbm, hbm, vmem, hbm],
        out_specs=vmem,
        scratch_shapes=[
            pltpu.VMEM((16, 72, 3 * HD), BF),
            pltpu.VMEM((16, 36, D), BF),
            pltpu.VMEM((16, 72, 3 * HD), BF),
            pltpu.VMEM((16, 36, D), BF),
            pltpu.VMEM((3, D, HP), BF),
            pltpu.VMEM((3, D, HP), BF),
            pltpu.VMEM((HP, D), BF),
            pltpu.VMEM((HP, D), BF),
            pltpu.VMEM((HP, 128), BF),
            pltpu.VMEM((256, HP), BF),
            pltpu.VMEM((8, HP), F32),
            pltpu.VMEM((8, 128), F32),
            pltpu.VMEM((TOK, D), BF),
            pltpu.VMEM((5, TOK, D), BF),
            pltpu.VMEM((TOK, HP), BF),
            pltpu.VMEM((10 * COLS, ROWS, HP), BF),
            pltpu.VMEM((10 * COLS, ROWS, HP), BF),
            pltpu.VMEM((8 * TOK, HP), BF),
            pltpu.VMEM((8 * TOK, HP), BF),
            pltpu.VMEM((TOK, HP), F32),
            pltpu.VMEM((TOK, D), BF),
            pltpu.VMEM((TOK, D), BF),
            pltpu.VMEM((TOK, D), BF),
            pltpu.VMEM((3, TOK, HP), BF),
            pltpu.VMEM((TOK, HP), BF),
            pltpu.VMEM((TOK, HP), BF),
            dma((4, 16)),
            dma((4, 16)),
            dma((4, 2)),
            dma((4, 2)),
            dma((2, 4)),
            dma((2, 4)),
            dma((16,)),
            dma((16,)),
            dma((16,)),
            dma((16,)),
            dma((4,)),
        ],
        compiler_params=pltpu.CompilerParams(
            collective_id=0, has_side_effects=True, vmem_limit_bytes=56 << 20
        ),
        cost_estimate=pl.CostEstimate(
            flops=10 * 10**9, bytes_accessed=4 * 10**6, transcendentals=5 * 10**6
        ),
    )(
        latent.reshape(TOK, D),
        timestep,
        modulation,
        window_offset,
        intersection_weight,
        spatial_in,
        spatial_gain,
        spatial_out,
        temporal_in,
        temporal_gain,
        temporal_out,
    )
    return out.reshape(latent.shape)


def solution(mesh):
    in_specs = (
        P("tm", None, "lon", None),
        P(),
        P(),
        P("tm"),
        P(),
        P("tm", None),
        P(),
        P("tm", None),
        P("tm", None),
        P(),
        P("tm", None),
    )
    out_specs = P("tm", None, "lon", None)
    return jax.shard_map(local, mesh=mesh, in_specs=in_specs, out_specs=out_specs, check_vma=False)
```

time: 497 us -> 135 us (0.27)
  the two profiles are of different devices: /device:TPU:18 before, /device:TPU:1 now
where the time goes in v1:
time: 135 us; the launch traced here: 134 us
  Pallas kernels  128 us (95%)
  local copies, waits for them, and re-layouts  4.58 us (3%)
    pallas_call x1, Pallas kernels, local(): pl.pallas_call(kernel, out_shape=jax.ShapeDtypeStruct((TOK, D), BF), in_s...  128 us
    unnamed x2, local copies, waits for them, and re-layouts  4.58 us

profile of v1, /device:TPU:1, one launch (start us, length us, event | category | flops | bytes accessed | tf_op | source)
XLA Modules:
  0.0 134.2 jit_solution(18279874925902079943)
XLA Ops:
  1.3 2.7 %copy.12.mod_ref = f32[30,6,1152]{2,1,0:T(8,128)} copy(f32[30,6,1152]{2,0,1:T(8,128)} %param.13) | data formatting | bytes 1658880 | tf_op args[2]
  4.0 128.4 %shard_map.109 = bf16[256,1152]{1,0:T(8,128)(2,1)} custom-call(bf16[256,1152]{1,0:T(8,128)(2,1)} %bitcast.3, s32[1]{0:T(128)S(6)} %copy.14.ts_ref, f32[30,6,1152]{2,1,0:T(8,128)} %copy.12.mod_ref, s32[1]{0:T(128)S(6)} %copy.15.off_ref, s32[32,32]{1,0:T(8,128)} %iw_ref.1, bf16[72,1728]{1,0:T(8,128)(2,1)} %si_ref.1, f32[2,72]{1,0:T(2,128)} %sg_ref.1, ...), custom_call_target="tpu_custom_call" | custom-call | flops 10000000000 | bytes 4000000 | tf_op jit(solution)/shard_map/pallas_call | solution.py:484
  132.3 1.9 %copy.16 = bf16[1,32,8,1152]{3,2,1,0:T(8,128)(2,1)} copy(bf16[1,32,8,1152]{3,2,1,0:T(8,128)(2,1)} %bitcast.2) | data formatting | bytes 1179648

commit v2 on v1

--- a/solution.py
+++ b/solution.py
@@ -119,6 +119,73 @@
         copy.start()
         sent.append(copy)
 
+    pair = dev(z * 2 + 1 - xl, l)
+
+    def ring_slot(k, plane, way):
+        return lax.rem(z - way * k + 2 * nz, nz) * 2 + plane
+
+    def ring_start(a):
+        own[a].wait()
+        send(a, t, 0, zn)
+
+        @pl.when(c == a)
+        def _():
+            wcopy(a, t, 17, pair).start()
+
+    def ring(a, k, other):
+        slot = ring_slot(k, 1 - xl if other else xl, d)
+        keeper = c == (1 if other else 0)
+        arrived = wcopy(a, slot, 0, zn)
+        onward = wcopy(a, slot, 4 * other + k if other else k, zn)
+        across = wcopy(a, slot, 7 + 4 * other + k, sib)
+        if k == 4:
+
+            @pl.when(keeper)
+            def _():
+                arrived.wait_recv()
+                across.start()
+
+        elif k == 3:
+            arrived.wait_recv()
+
+            @pl.when(keeper)
+            def _():
+                onward.start()
+
+            across.start()
+            sent.append(across)
+        elif k == 0:
+            arrived.wait_recv()
+            onward.start()
+            sent.append(onward)
+            across = wcopy(a, slot, 16, sib)
+
+            @pl.when(c == a)
+            def _():
+                across.start()
+
+        else:
+            arrived.wait_recv()
+            onward.start()
+            across.start()
+            sent.extend((onward, across))
+
+    def ring_rest(a):
+        for other in (0, 1):
+            for k in range(1, 4):
+                slot = ring_slot(k, 1 - xl if other else xl, -d)
+                wcopy(a, slot, 0, zn).wait_recv()
+        wcopy(a, ring_slot(4, lax.rem(xl + 1 - c, 2), d), 0, zn).wait_recv()
+
+    def ring_end(a):
+        @pl.when(c == a)
+        def _():
+            wcopy(a, t, 17, pair).wait_send()
+            wcopy(a, t, 16, sib).wait_send()
+
+        wcopy(a, t, 3 + 4 * c, zn).wait_send()
+        wcopy(a, t, 11 + 4 * c, sib).wait_send()
+
     def gather_start(a):
         own[a].wait()
 
@@ -126,6 +193,11 @@
         def _():
             wcopy(a, t, 3, zn).start()
 
+        @pl.when(c == 0)
+        def _():
+            wcopy(a, t, 0, zn).start()
+            wcopy(a, t, 4, xn).start()
+
     def gather_a(a, i):
         slot = mine(i, xl)
         if i == 0:
@@ -133,14 +205,16 @@
             @pl.when(c == 1)
             def _():
                 wcopy(a, slot, 0, zn).wait_recv()
+                wcopy(a, slot, 0, zn).start()
+                wcopy(a, slot, 4, xn).start()
                 wcopy(a, slot, 8, sib).start()
 
-        else:
-            wcopy(a, slot, 0, zn).wait_recv()
-            send(a, slot, 8 + i, sib)
+            return
+        wcopy(a, slot, 0, zn).wait_recv()
         if i < 3:
             send(a, slot, i, zn)
         send(a, slot, 4 + i, xn)
+        send(a, slot, 8 + i, sib)
 
     def gather_b(a, i):
         slot = mine(i, 1 - xl)
@@ -161,6 +235,9 @@
             wcopy(a, theirs(i, 1 - xl), 0, zn).wait_recv()
 
     def gather_end(a):
+        wcopy(a, mine(0, xl), 0, zn).wait_send()
+        wcopy(a, mine(0, xl), 4, xn).wait_send()
+
         @pl.when(c == 1)
         def _():
             wcopy(a, t, 3, zn).wait_send()
@@ -184,12 +261,12 @@
             target[144 * four : 144 * (four + 1), :] = block.astype(BF)
         target[HD:HP, :] = jnp.zeros((HP - HD, D), BF)
 
-    gather_start(0)
-    gather_a(0, 0)
-
-    steps = mod_ref.shape[0]
-    chosen = (iota((steps, 6, D), 0) == ts_ref[0]).astype(F32)
-    modulators = jnp.sum(mod_ref[...] * chosen, axis=0)
+    ring_start(0)
+    ring_start(1)
+
+    steps = mod_ref.shape[1]
+    chosen = (iota((6, steps, D), 1) == ts_ref[0]).astype(F32)
+    modulators = jnp.sum(mod_ref[...] * chosen, axis=1)
     there = iota((TOK, TOK), 1)
     here = iota((TOK, TOK), 0)
     perm = (there == (here & 31) * COLS + (here >> 5)).astype(F32).astype(BF)
@@ -197,29 +274,25 @@
     latp[...] = ordered.astype(BF)
     xs[2] = (layer_norm(ordered) * (1.0 + modulators[1:2]) + modulators[0:1]).astype(BF)
 
-    HALF = TOK // 2
-
-    def scopy(source, hop, side, half):
-        part = pl.ds(half * HALF, HALF)
-        slot = 2 - hop if side == 0 else 2 + hop
+    def scopy(source, hop, side):
         return pltpu.make_async_remote_copy(
-            src_ref=xs.at[source, part], dst_ref=xs.at[slot, part],
-            send_sem=s_send.at[2 * (hop - 1) + side, half],
-            recv_sem=s_recv.at[2 * (hop - 1) + side, half],
+            src_ref=xs.at[source], dst_ref=xs.at[2 - hop if side == 0 else 2 + hop],
+            send_sem=s_send.at[2 * (hop - 1) + side], recv_sem=s_recv.at[2 * (hop - 1) + side],
             device_id=east if side == 0 else west, device_id_type=MESH,
         )
 
-    def strip_send(hop, half):
+    def strip_send(hop):
         for side in (0, 1):
             source = 2 if hop == 1 else (1 if side == 0 else 3)
             if hop == 2:
-                scopy(2, 1, side, half).wait_recv()
-            copy = scopy(source, hop, side, half)
+                scopy(2, 1, side).wait_recv()
+            copy = scopy(source, hop, side)
             copy.start()
             sent.append(copy)
 
-    strip_send(1, 0)
-    strip_send(1, 1)
+    ring(0, 1, 0)
+    ring(0, 0, 1)
+    strip_send(1)
 
     kbuf[9 * COLS :] = jnp.zeros((COLS, ROWS, HP), BF)
     vbuf[9 * COLS :] = jnp.zeros((COLS, ROWS, HP), BF)
@@ -243,31 +316,24 @@
     )
     factor = HEAD_DIM ** (-0.5) * LOG2E
 
-    gather_a(0, 1)
-    gather_b(0, 0)
-    gather_a(0, 2)
-    gather_b(0, 1)
-    strip_send(2, 0)
-    gather_a(0, 3)
-    gather_b(0, 2)
-    gather_start(1)
-    gather_a(1, 0)
-    strip_send(2, 1)
-    gather_b(0, 3)
-    gather_a(1, 1)
-    gather_b(1, 0)
-    gather_a(1, 2)
-    gather_b(1, 1)
-    gather_rest(0)
-    gather_start(2)
-    gather_start(3)
-    gather_a(2, 0)
-    gather_a(3, 0)
+    ring(0, 2, 0)
+    ring(1, 1, 0)
+    ring(0, 1, 1)
+    ring(1, 0, 1)
+    ring(0, 3, 0)
+    ring(1, 2, 0)
+    strip_send(2)
+    ring(0, 2, 1)
+    ring(1, 1, 1)
+    ring(0, 4, 0)
+    ring(0, 3, 1)
+    ring(1, 3, 0)
+    ring(1, 2, 1)
+    ring(0, 4, 1)
+    ring_rest(0)
     arrange_in(w_si, w_spat)
 
     qbuf[...] = head_norm(dot(xs[2], w_spat[0]), gains[0:1] * factor, seg[...], seg_t[...])
-    gather_a(1, 3)
-    gather_b(1, 2)
 
     def keys_values(slot):
         cols = pl.ds(slot * (2 * COLS), COLS)
@@ -294,33 +360,36 @@
             copy.start()
             sent.append(copy)
 
-    @pl.loop(0, 3)
-    def _(i):
-        keys_values(2 - lax.rem(i, 2) + i // 2)
+    keys_values(2)
+    ring(1, 4, 0)
+    ring(1, 3, 1)
+    later = (2, 3)
+    for a in later:
+        gather_start(a)
+    keys_values(1)
+    ring(1, 4, 1)
+    keys_values(3)
 
     kv_share(1)
     kv_share(2)
     kv_share(3 * c)
-    gather_b(1, 3)
-    gather_rest(1)
-    arrange_out(w_so, wo_spat)
-    gather_a(2, 1)
-    gather_a(3, 1)
-    gather_b(2, 0)
-    gather_b(3, 0)
-    for half in (0, 1):
-        for side in (0, 1):
-            scopy(2, 2, side, half).wait_recv()
-
-    @pl.loop(0, 2)
-    def _(i):
-        keys_values(4 * i)
+
+    def hop(i):
+        for a in later:
+            if i < 4:
+                gather_a(a, i)
+        for a in later:
+            if i > 0:
+                gather_b(a, i - 1)
+
+    hop(0)
+    for side in (0, 1):
+        scopy(2, 2, side).wait_recv()
+    keys_values(0)
+    keys_values(4)
 
     kv_share(3 - 3 * c)
-    gather_a(2, 2)
-    gather_a(3, 2)
-    gather_b(2, 1)
-    gather_b(3, 1)
+    hop(1)
 
     shift = lax.rem(COLS * l - off_ref[0] + STRIDE, STRIDE)
     table = iw_ref[...].astype(F32)
@@ -347,7 +416,7 @@
         vcell[rows, :] = vbuf[col + STRIDE - shift]
 
     def window(h):
-        w = pl.multiple_of(((9 * h) // 16) * 128, 128)
+        w = (9 * h) // 16 * 128
         off = HEAD_DIM * h - w
         lanes = iota((1, 256), 1)
         inside = ((lanes >= off) & (lanes < off + HEAD_DIM)).astype(F32)
@@ -380,14 +449,14 @@
         return 0
 
     att[...] = jnp.zeros_like(att)
-    lax.fori_loop(0, 4, spatial_head, 0)
-    gather_a(2, 3)
-    gather_a(3, 3)
-    gather_b(2, 2)
-    gather_b(3, 2)
-    lax.fori_loop(4, 8, spatial_head, 0)
-    gather_b(2, 3)
-    gather_b(3, 3)
+    for h in range(4):
+        spatial_head(h, 0)
+    hop(2)
+    for h in range(4, 8):
+        spatial_head(h, 0)
+    hop(3)
+    ring_rest(1)
+    arrange_out(w_so, wo_spat)
 
     middle = latp[...].astype(F32) + modulators[2:3] * dot(att[...].astype(BF), wo_spat[...])
     middle = middle.astype(BF)
@@ -423,6 +492,8 @@
             ).wait_recv()
 
     exchange(nm, xt, a_send, a_recv)
+    for a in (2, 3):
+        gather_b(a, 3)
     gather_rest(2)
     gather_rest(3)
     arrange_in(w_ti, w_temp)
@@ -447,7 +518,8 @@
         return 0
 
     att[...] = jnp.zeros_like(att)
-    lax.fori_loop(0, 8, temporal_head, 0)
+    for h in range(8):
+        temporal_head(h, 0)
     tsend[...] = att[...].astype(BF)
     exchange(tsend, rt, r_send, r_recv)
     there = iota((TOK, TOK), 1)
@@ -460,7 +532,9 @@
 
     for copy in sent:
         copy.wait_send()
-    for a in range(4):
+    for a in (0, 1):
+        ring_end(a)
+    for a in later:
         gather_end(a)
 
 
@@ -513,10 +587,10 @@
             pltpu.VMEM((3, TOK, HP), BF),
             pltpu.VMEM((TOK, HP), BF),
             pltpu.VMEM((TOK, HP), BF),
+            dma((4, 18)),
             dma((4, 16)),
-            dma((4, 16)),
-            dma((4, 2)),
-            dma((4, 2)),
+            dma((4,)),
+            dma((4,)),
             dma((2, 4)),
             dma((2, 4)),
             dma((16,)),
@@ -534,7 +608,7 @@
     )(
         latent.reshape(TOK, D),
         timestep,
-        modulation,
+        jnp.transpose(modulation, (1, 0, 2)),
         window_offset,
         intersection_weight,
         spatial_in,

time: 135 us -> 110 us (0.81)
  Pallas kernels: 128 us -> 107 us
  local copies, waits for them, and re-layouts: 4.58 us -> 1.92 us
    pallas_call x1, Pallas kernels: 128 us -> 107 us  [local(): pl.pallas_call(kernel, out_shape=jax.ShapeDtypeStruct((TOK, D), BF), in_s...]
    unnamed x2 -> x1, local copies, waits for them, and re-layouts: 4.58 us -> 1.92 us
where the time goes in v2:
time: 110 us
  Pallas kernels  107 us (97%)
  local copies, waits for them, and re-layouts  1.92 us (2%)
  between operations  1.31 us (1%)
    pallas_call x1, Pallas kernels, local(): pl.pallas_call(kernel, out_shape=jax.ShapeDtypeStruct((TOK, D), BF), in_s...  107 us

profile of v2, /device:TPU:1, one launch (start us, length us, event | category | flops | bytes accessed | tf_op | source)
XLA Modules:
  0.0 109.9 jit_solution(12076844119181233890)
XLA Ops:
  1.3 106.7 %shard_map.109 = bf16[256,1152]{1,0:T(8,128)(2,1)} custom-call(bf16[256,1152]{1,0:T(8,128)(2,1)} %bitcast.5, s32[1]{0:T(128)S(6)} %copy.13.ts_ref, f32[6,30,1152]{2,1,0:T(8,128)} %bitcast.4, s32[1]{0:T(128)S(6)} %copy.14.off_ref, s32[32,32]{1,0:T(8,128)} %iw_ref.1, bf16[72,1728]{1,0:T(8,128)(2,1)} %si_ref.1, f32[2,72]{1,0:T(2,128)} %sg_ref.1, ...), custom_call_target="tpu_custom_call" | custom-call | flops 10000000000 | bytes 4000000 | tf_op jit(solution)/shard_map/pallas_call | solution.py:558
  108.0 1.9 %copy.15 = bf16[1,32,8,1152]{3,2,1,0:T(8,128)(2,1)} copy(bf16[1,32,8,1152]{3,2,1,0:T(8,128)(2,1)} %bitcast.3) | data formatting | bytes 1179648

commit v3 on v2

--- a/solution.py
+++ b/solution.py
@@ -454,7 +454,6 @@
     hop(2)
     for h in range(4, 8):
         spatial_head(h, 0)
-    hop(3)
     ring_rest(1)
     arrange_out(w_so, wo_spat)
 
@@ -492,6 +491,7 @@
             ).wait_recv()
 
     exchange(nm, xt, a_send, a_recv)
+    hop(3)
     for a in (2, 3):
         gather_b(a, 3)
     gather_rest(2)

time: 110 us -> 107 us (0.973)
  Pallas kernels: 107 us -> 104 us
    pallas_call x1, Pallas kernels: 107 us -> 104 us  [local(): pl.pallas_call(kernel, out_shape=jax.ShapeDtypeStruct((TOK, D), BF), in_s...]
where the time goes in v3:
time: 107 us
  Pallas kernels  104 us (97%)
  local copies, waits for them, and re-layouts  1.92 us (2%)
  between operations  1.31 us (1%)
    pallas_call x1, Pallas kernels, local(): pl.pallas_call(kernel, out_shape=jax.ShapeDtypeStruct((TOK, D), BF), in_s...  104 us

profile of v3, /device:TPU:1, one launch (start us, length us, event | category | flops | bytes accessed | tf_op | source)
XLA Modules:
  0.0 107.1 jit_solution(10062701187668997482)
XLA Ops:
  1.3 103.9 %shard_map.109 = bf16[256,1152]{1,0:T(8,128)(2,1)} custom-call(bf16[256,1152]{1,0:T(8,128)(2,1)} %bitcast.5, s32[1]{0:T(128)S(6)} %copy.13.ts_ref, f32[6,30,1152]{2,1,0:T(8,128)} %bitcast.4, s32[1]{0:T(128)S(6)} %copy.14.off_ref, s32[32,32]{1,0:T(8,128)} %iw_ref.1, bf16[72,1728]{1,0:T(8,128)(2,1)} %si_ref.1, f32[2,72]{1,0:T(2,128)} %sg_ref.1, ...), custom_call_target="tpu_custom_call" | custom-call | flops 10000000000 | bytes 4000000 | tf_op jit(solution)/shard_map/pallas_call | solution.py:558
  105.2 1.9 %copy.15 = bf16[1,32,8,1152]{3,2,1,0:T(8,128)(2,1)} copy(bf16[1,32,8,1152]{3,2,1,0:T(8,128)(2,1)} %bitcast.3) | data formatting | bytes 1179648
